TPU v7x, 32 devices: a whole 2x2x4 slice. The times are simulated.
32 devices in a mesh: parts: 2 (over y), seq: 4 (over z), head: 2 (over x), sub: 2 (over core).
Axes of the slice: x: 2, y: 2, z: 4, core: 2. Of those that a mesh axis runs over, the one named last changes fastest.
Arguments:
- queries: bfloat16 [8192, 8192], P(('parts', 'seq'), ('head', 'sub')), parts along dimension 0, may hold values from -7 to 7
- keys: bfloat16 [8192, 1024], P(('parts', 'seq'), 'head'), parts along dimension 0, may hold values from -4 to 4
- values: bfloat16 [8192, 1024], P(('parts', 'seq'), 'head'), parts along dimension 0, may hold values from -5 to 5
- out_grad: bfloat16 [8192, 8192], P(('parts', 'seq'), ('head', 'sub')), parts along dimension 0, may hold values from -12 to 12
- prompt_group: int32 [8], P('parts'), parts along dimension 0, may hold values from 0 to 3, each once
- slot_group: int32 [8, 2], P('parts'), parts along dimension 0, may hold values from 0 to 3, as said below
- resp_len: int32 [8, 2], P(('parts', 'seq')), parts along dimension 0, may hold values from 128 to 256, as said below
Outputs:
- query_grad: bfloat16 [8192, 8192], P(('parts', 'seq'), ('head', 'sub')), parts along dimension 0
- key_grad: bfloat16 [8192, 1024], P(('parts', 'seq'), 'head'), parts along dimension 0
- value_grad: bfloat16 [8192, 1024], P(('parts', 'seq'), 'head'), parts along dimension 0
There are 2 independent parts, one for each index of `parts`. A program takes and returns all parts, laid end to end along the dimension named above; each array names one. Nothing has to cross between parts.
Inputs may be any that keep to these rules, and one draw needn't show every extreme that they name: `slot_group`: each group id appears in exactly two of the 8 slots. `resp_len`: some slot has exactly 256. `prompt_group`: each group's prompt is in exactly one block.
All inputs are finite; a program needn't handle non-finite values.
Results may differ from a plain program's by a relative error of at most 0.0088.
Values may be sent and summed in bfloat16 or wider, within the bound.
A program may use at most 128 MiB of HBM per device.

v0:
```python
import functools
import math

import jax
import jax.numpy as jnp
from jax import lax
from jax.experimental import pallas as pl
from jax.experimental.pallas import tpu as pltpu
from jax.sharding import PartitionSpec as P

HQ = 64
KVH = 8
HD = 128
PROMPT = 512
RESP = 256
SCALE = 1.0 / math.sqrt(HD)
EXP2_SCALE = SCALE * math.log2(math.e)
ROW_ROW = (((1,), (1,)), ((), ()))
COL_COL = (((0,), (0,)), ((), ()))


def attend(query, grad, key, value):
    extent, amount = key.shape[0], query.shape[0]
    scores = lax.dot_general(key, query, ROW_ROW, preferred_element_type=jnp.float32)
    grad_chance = lax.dot_general(value, grad, ROW_ROW, preferred_element_type=jnp.float32)
    key_index = lax.broadcasted_iota(jnp.int32, (amount, amount), 0)
    query_index = lax.broadcasted_iota(jnp.int32, (amount, amount), 1)
    last = jnp.where(key_index <= query_index, scores[extent - amount :], -jnp.inf)
    if extent > amount:
        scores = jnp.concatenate([scores[: extent - amount], last], axis=0)
    else:
        scores = last
    highest = jnp.max(scores, axis=0, keepdims=True)
    weights = jnp.exp2((scores - highest) * EXP2_SCALE)
    inverse = 1.0 / jnp.sum(weights, axis=0, keepdims=True)
    row_dot = jnp.sum(weights * grad_chance, axis=0, keepdims=True) * inverse
    chances = (weights * inverse).astype(jnp.bfloat16)
    grad_score = chances * (grad_chance - row_dot).astype(jnp.bfloat16)
    key_term = jnp.dot(grad_score, query, preferred_element_type=jnp.float32) * SCALE
    value_term = jnp.dot(chances, grad, preferred_element_type=jnp.float32)
    query_turned = lax.dot_general(key, grad_score, COL_COL, preferred_element_type=jnp.float32)
    query_grad = (query_turned.T * SCALE).astype(jnp.bfloat16)
    return query_grad, key_term, value_term


def prompt_kernel(shared, table, q_ref, g_ref, k_ref, v_ref, dq_ref, dk_ref, dv_ref):
    @pl.when(pl.program_id(0) % shared == 0)
    def _():
        dk_ref[...] = jnp.zeros_like(dk_ref)
        dv_ref[...] = jnp.zeros_like(dv_ref)

    for begin in range(0, PROMPT, RESP):
        rows = pl.ds(begin, RESP)
        seen = pl.ds(0, begin + RESP)
        dq, dk, dv = attend(q_ref[rows, :], g_ref[rows, :], k_ref[seen, :], v_ref[seen, :])
        dq_ref[rows, :] = dq
        dk_ref[seen, :] += dk
        dv_ref[seen, :] += dv


def reply_kernel(
    shared, table, q_ref, g_ref, k_ref, v_ref, pk0, pv0, pk1, pv1, _, dq_ref, out_ref, dk_ref, dv_ref, kacc, vacc
):
    step = pl.program_id(0) % shared

    @pl.when(step == 0)
    def _():
        kacc[...] = jnp.zeros_like(kacc)
        vacc[...] = jnp.zeros_like(vacc)

    index = lax.broadcasted_iota(jnp.int32, (RESP, 1), 0)
    for slot in range(2):
        rows = pl.ds(slot * RESP, RESP)
        prompt_key, prompt_value = ((pk0, pv0), (pk1, pv1))[slot]
        grad = jnp.where(index < table[3 + slot], g_ref[rows, :], jnp.zeros((), jnp.bfloat16))
        key = jnp.concatenate([prompt_key[0], k_ref[rows, :]], axis=0)
        value = jnp.concatenate([prompt_value[0], v_ref[rows, :]], axis=0)
        dq, dk, dv = attend(q_ref[rows, :], grad, key, value)
        dq_ref[rows, :] = dq
        kacc[slot] += dk
        vacc[slot] += dv

    @pl.when(step == shared - 1)
    def _():
        for slot in range(2):
            rows = pl.ds(slot * RESP, RESP)
            dk_ref[rows, :] = kacc[slot, PROMPT:]
            dv_ref[rows, :] = vacc[slot, PROMPT:]
        for peer in range(out_ref.shape[0]):
            for column, acc in ((0, kacc), (HD, vacc)):
                first = jnp.where(table[1] == peer, acc[0, :PROMPT], 0.0)
                second = jnp.where(table[2] == peer, acc[1, :PROMPT], 0.0)
                out_ref[peer, :, column : column + HD] = (first + second).astype(jnp.bfloat16)


def per_device(queries, keys, values, out_grad, prompt_group, slot_group, resp_len):
    seq_count = lax.axis_size("seq")
    local_heads = queries.shape[1] // HD
    kv_local = keys.shape[1] // HD
    used = max(local_heads // (HQ // KVH), 1)
    shared = local_heads // used
    first_head = lax.axis_index("sub") * local_heads // (HQ // KVH) if used != kv_local else 0
    if used == kv_local:
        key_part, value_part = keys[:PROMPT], values[:PROMPT]
    else:
        key_part = lax.dynamic_slice(keys, (0, first_head * HD), (PROMPT, used * HD))
        value_part = lax.dynamic_slice(values, (0, first_head * HD), (PROMPT, used * HD))
    prompt_pair = jnp.concatenate([key_part, value_part], axis=1)
    every = lax.all_gather(prompt_pair[None], "seq", axis=0, tiled=True)
    peers = jnp.arange(seq_count, dtype=jnp.int32)
    owners = jnp.sum(
        peers[:, None] * (prompt_group[:, None] == peers[None, :]).astype(jnp.int32), axis=0
    )
    own_index = lax.axis_index("seq")
    my_slots = jnp.sum(slot_group * (peers[:, None] == own_index).astype(jnp.int32), axis=0)
    my_owner = jnp.sum(
        owners[None, :] * (my_slots[:, None] == peers[None, :]).astype(jnp.int32), axis=1
    )
    table = jnp.concatenate(
        [jnp.full((1,), first_head, jnp.int32), my_owner, resp_len[0]]
    ).astype(jnp.int32)

    def head_block(row):
        return pl.BlockSpec((PROMPT, HD), lambda h, t: (row, h))

    def kv_block(row):
        return pl.BlockSpec((PROMPT, HD), lambda h, t: (row, t[0] + h // shared))

    sum_block = pl.BlockSpec((PROMPT, HD), lambda h, t: (0, h // shared))

    def fetched_block(slot, offset):
        return pl.BlockSpec((1, PROMPT, HD), lambda h, t: (t[1 + slot], 0, offset + h // shared))

    params = pltpu.CompilerParams(
        dimension_semantics=("arbitrary",), vmem_limit_bytes=40 * 1024 * 1024
    )
    grad_shape = jax.ShapeDtypeStruct((PROMPT, used * HD), jnp.float32)
    query_shape = jax.ShapeDtypeStruct(queries.shape, jnp.bfloat16)
    work = local_heads * RESP * RESP * HD * 10
    query_half, prompt_dk, prompt_dv = pl.pallas_call(
        functools.partial(prompt_kernel, shared),
        grid_spec=pltpu.PrefetchScalarGridSpec(
            num_scalar_prefetch=1,
            grid=(local_heads,),
            in_specs=[head_block(0), head_block(0), kv_block(0), kv_block(0)],
            out_specs=[head_block(0), sum_block, sum_block],
        ),
        out_shape=[query_shape, grad_shape, grad_shape],
        compiler_params=params,
        cost_estimate=pl.CostEstimate(
            flops=work * 3 * 2, bytes_accessed=8 << 20, transcendentals=0
        ),
    )(table, queries, out_grad, keys, values)
    query_total, outgoing, reply_dk, reply_dv = pl.pallas_call(
        functools.partial(reply_kernel, shared),
        grid_spec=pltpu.PrefetchScalarGridSpec(
            num_scalar_prefetch=1,
            grid=(local_heads,),
            in_specs=[head_block(1), head_block(1), kv_block(1), kv_block(1)]
            + [fetched_block(slot, offset) for slot in range(2) for offset in (0, used)]
            + [pl.BlockSpec(memory_space=pl.ANY)],
            out_specs=[
                head_block(1),
                pl.BlockSpec((seq_count, PROMPT, 2 * HD), lambda h, t: (0, 0, h // shared)),
                sum_block,
                sum_block,
            ],
            scratch_shapes=[pltpu.VMEM((2, PROMPT + RESP, HD), jnp.float32)] * 2,
        ),
        out_shape=[
            query_shape,
            jax.ShapeDtypeStruct((seq_count, PROMPT, used * 2 * HD), jnp.bfloat16),
            grad_shape,
            grad_shape,
        ],
        input_output_aliases={9: 0},
        compiler_params=params,
        cost_estimate=pl.CostEstimate(
            flops=work * 6 * 2, bytes_accessed=8 << 20, transcendentals=0
        ),
    )(table, queries, out_grad, keys, values, every, every, every, every, query_half)
    arrived = lax.all_to_all(outgoing, "seq", split_axis=0, concat_axis=0, tiled=True)
    returned = jnp.sum(arrived.astype(jnp.float32), axis=0).reshape(PROMPT, used, 2, HD)
    key_top = prompt_dk + returned[:, :, 0].reshape(PROMPT, used * HD)
    value_top = prompt_dv + returned[:, :, 1].reshape(PROMPT, used * HD)

    def across(rows):
        mine = rows.astype(jnp.bfloat16)
        if used == kv_local:
            return lax.psum(mine, "sub").astype(jnp.bfloat16)
        other = lax.ppermute(mine, "sub", [(0, 1), (1, 0)])
        front = lax.axis_index("sub") == 0
        return jnp.concatenate(
            [jnp.where(front, mine, other), jnp.where(front, other, mine)], axis=1
        )

    top = across(jnp.concatenate([key_top, value_top], axis=0))
    low = across(jnp.concatenate([reply_dk, reply_dv], axis=0))
    key_total = jnp.concatenate([top[:PROMPT], low[:PROMPT]], axis=0)
    value_total = jnp.concatenate([top[PROMPT:], low[PROMPT:]], axis=0)
    return (query_total, key_total, value_total)


def solution(mesh):
    placed = (
        P(("parts", "seq"), ("head", "sub")),
        P(("parts", "seq"), "head"),
        P(("parts", "seq"), "head"),
        P(("parts", "seq"), ("head", "sub")),
        P("parts"),
        P("parts", None),
        P(("parts", "seq"), None),
    )
    return jax.shard_map(
        per_device,
        mesh=mesh,
        in_specs=placed,
        out_specs=(
            P(("parts", "seq"), ("head", "sub")),
            P(("parts", "seq"), "head"),
            P(("parts", "seq"), "head"),
        ),
        check_vma=False,
    )
```

profile of v0, /device:TPU:0, one launch (start us, length us, event | category | flops | bytes accessed | tf_op | source)
XLA Modules:
  0.0 167.9 jit_solution(7112257246869606282)
XLA Ops:
  7.2 0.0 copy-start.1
  7.2 0.0 copy-start
  7.2 0.0 copy-start.10
  7.2 0.0 copy-start.12
  7.2 0.0 copy-start.11
  7.2 0.0 all-gather.3.cloned.1.call-start
  7.3 1.2 constant_dynamic-slice_fusion
  8.5 0.8 pad_maximum_fusion.2
  9.3 0.0 all-gather.3.cloned.1.call-update
  9.4 0.0 copy-done.10
  9.4 0.1 multiply_reduce_fusion
  9.5 0.0 copy-done.12
  9.5 0.1 select_reduce_fusion
  9.6 0.2 fusion.6
  9.8 0.0 copy-done.11
  9.8 0.1 pad_add_fusion.table
  9.8 0.0 copy-done.1
  9.8 0.0 copy-done
  9.8 0.0 copy-start.3
  9.9 2.2 %copy-done.3 = bf16[1024,2048]{1,0:T(8,128)(2,1)S(1)} copy-done((bf16[1024,2048]{1,0:T(8,128)(2,1)S(1)}, bf16[1024,2048]{1,0:T(8,128)(2,1)}, u32[]{:S(2)}) %copy-start.3) | copy-done | bytes 4194328
  12.0 0.0 copy-start.5
  12.0 2.2 %copy-done.5 = bf16[1024,2048]{1,0:T(8,128)(2,1)S(1)} copy-done((bf16[1024,2048]{1,0:T(8,128)(2,1)S(1)}, bf16[1024,2048]{1,0:T(8,128)(2,1)}, u32[]{:S(2)}) %copy-start.5) | copy-done | bytes 4194328
  14.2 22.8 %shard_map.94 = (bf16[1024,2048]{1,0:T(8,128)(2,1)}, f32[512,256]{1,0:T(8,128)S(1)}, f32[512,256]{1,0:T(8,128)S(1)}) custom-call(s32[5]{0:T(128)S(1)} %pad_add_fusion.table, bf16[1024,2048]{1,0:T(8,128)(2,1)S(1)} %copy-done.3, bf16[1024,2048]{1,0:T(8,128)(2,1)S(1)} %copy-done.5, bf16[1024,512]{1,0:T(8,128)(2,1)S(1)} %copy-done, bf16[1024,512]{1,0:T(8,128)(2,1)S(1)} %copy-done.1), custom_call_target="tpu_custom_call" | custom-call | flops 8053063680 | bytes 8388608 | tf_op jit(solution)/shard_map/pallas_call | solution.py:140
  37.0 21.8 %all-gather.3.cloned.1.call-done = bf16[2048,512]{1,0:T(8,128)(2,1)} async-done(((bf16[512,512]{1,0:T(8,128)(2,1)}), bf16[2048,512]{1,0:T(8,128)(2,1)}) %all-gather.3.cloned.1.call-update) | async-done | bytes 2097168 | tf_op jit(solution)/shard_map/all_gather | solution.py:109
  58.9 0.0 copy-start.2
  58.9 1.2 copy-done.2
  60.1 0.0 copy-start.4
  60.1 2.2 %copy-done.4 = bf16[1024,2048]{1,0:T(8,128)(2,1)S(1)} copy-done((bf16[1024,2048]{1,0:T(8,128)(2,1)S(1)}, bf16[1024,2048]{1,0:T(8,128)(2,1)}, u32[]{:S(2)}) %copy-start.4) | copy-done | bytes 4194328
  62.3 0.0 copy-start.6
  62.3 1.6 copy-done.6
  63.9 35.2 %shard_map.95 = (bf16[1024,2048]{1,0:T(8,128)(2,1)}, bf16[4,512,512]{2,1,0:T(8,128)(2,1)}, f32[512,256]{1,0:T(8,128)S(1)}, f32[512,256]{1,0:T(8,128)S(1)}) custom-call(s32[5]{0:T(128)S(1)} %pad_add_fusion.table, bf16[1024,2048]{1,0:T(8,128)(2,1)S(1)} %copy-done.4, bf16[1024,2048]{1,0:T(8,128)(2,1)} %g_ref.3, ...), custom_call_target="tpu_custom_call", output_to_operand_aliasing={{0}: (9, {})} | custom-call | flops 16106127360 | bytes 8388608 | tf_op jit(solution)/shard_map/pallas_call | solution.py:154
  99.1 4.4 %all-to-all-start = ((bf16[4,512,512]{2,1,0:T(8,128)(2,1)}), bf16[4,512,512]{2,1,0:T(8,128)(2,1)}, u32[]{:S(2)}, u32[]{:S(2)}) async-start(bf16[4,512,512]{2,1,0:T(8,128)(2,1)} %get-tuple-element.13), calls=%async_computation | async-start | bytes 4194304 | tf_op jit(solution)/shard_map/all_to_all | solution.py:182
  103.6 0.0 copy-start.7
  103.6 0.9 pad_maximum_fusion.4
  104.5 0.0 collective-permute-start.1
  104.5 0.0 copy-done.7
  104.5 47.6 %all-to-all-done = bf16[4,512,512]{2,1,0:T(8,128)(2,1)} async-done(((bf16[4,512,512]{2,1,0:T(8,128)(2,1)}), bf16[4,512,512]{2,1,0:T(8,128)(2,1)}, u32[]{:S(2)}, u32[]{:S(2)}) %all-to-all-start) | async-done | bytes 2097184 | tf_op jit(solution)/shard_map/all_to_all | solution.py:182
  152.1 2.0 %convert_reduce_fusion = f32[512,512]{1,0:T(8,128)S(1)} fusion(bf16[4,512,512]{2,1,0:T(8,128)(2,1)} %all-to-all-done), kind=kLoop, calls=%fused_computation | loop fusion | flops 1835008 | bytes 3145728 | tf_op jit(solution)/shard_map/reduce_sum | solution.py:183
  154.1 0.3 copy.16
  154.4 0.9 fusion.7
  155.3 0.0 copy-start.9
  155.3 0.2 copy.19
  155.5 0.0 copy-start.8
  155.6 0.1 add_convert_fusion.1
  155.6 0.7 copy-done.9
  156.4 0.2 copy.20
  156.6 0.1 add_convert_fusion
  156.7 0.1 collective-permute-start
  156.8 0.0 collective-permute-done.1
  156.8 0.0 copy-done.8
  156.8 1.2 broadcast_select_fusion
  158.1 0.6 collective-permute-done
  158.7 0.2 broadcast_select_fusion.2
  158.9 1.1 fusion.3
  160.0 1.0 pad_maximum_fusion.1
  (6 shorter events, 0.2 us)
Async XLA Ops:
  7.2 2.7 %copy-start.1 = (bf16[1024,512]{1,0:T(8,128)(2,1)S(1)}, bf16[1024,512]{1,0:T(8,128)(2,1)}, u32[]{:S(2)}) copy-start(bf16[1024,512]{1,0:T(8,128)(2,1)} %v_ref.3) | copy-start | bytes 3145732
  7.2 2.7 %copy-start = (bf16[1024,512]{1,0:T(8,128)(2,1)S(1)}, bf16[1024,512]{1,0:T(8,128)(2,1)}, u32[]{:S(2)}) copy-start(bf16[1024,512]{1,0:T(8,128)(2,1)} %k_ref.3) | copy-start | bytes 3145732
  7.2 2.2 %copy-start.10 = (s32[4,2]{0,1:T(2,128)S(1)}, s32[4,2]{0,1:T(2,128)}, u32[]{:S(2)}) copy-start(s32[4,2]{0,1:T(2,128)} %param.12) | copy-start | bytes 100
  7.2 2.3 %copy-start.12 = (s32[4]{0:T(128)S(1)}, s32[4]{0:T(128)}, u32[]{:S(2)}) copy-start(s32[4]{0:T(128)} %param.11) | copy-start | bytes 52
  7.2 2.6 %copy-start.11 = (s32[1,2]{1,0:T(1,128)S(1)}, s32[1,2]{1,0:T(1,128)}, u32[]{:S(2)}) copy-start(s32[1,2]{1,0:T(1,128)} %param.13) | copy-start | bytes 28
  7.2 51.6 %all-gather.3.cloned.1.call-start = ((), (), s32[]{:S(2)}) async-start(), calls=%async_computation.1 | async-start | bytes 2621440 | tf_op jit(solution)/shard_map/all_gather | solution.py:109
  9.8 2.2 %copy-start.3 = (bf16[1024,2048]{1,0:T(8,128)(2,1)S(1)}, bf16[1024,2048]{1,0:T(8,128)(2,1)}, u32[]{:S(2)}) copy-start(bf16[1024,2048]{1,0:T(8,128)(2,1)} %q_ref.3) | copy-start | bytes 12582916
  12.0 2.2 %copy-start.5 = (bf16[1024,2048]{1,0:T(8,128)(2,1)S(1)}, bf16[1024,2048]{1,0:T(8,128)(2,1)}, u32[]{:S(2)}) copy-start(bf16[1024,2048]{1,0:T(8,128)(2,1)} %g_ref.3) | copy-start | bytes 12582916
  58.9 1.2 copy-start.2
  60.1 2.2 %copy-start.4 = (bf16[1024,2048]{1,0:T(8,128)(2,1)S(1)}, bf16[1024,2048]{1,0:T(8,128)(2,1)}, u32[]{:S(2)}) copy-start(bf16[1024,2048]{1,0:T(8,128)(2,1)} %q_ref.3) | copy-start | bytes 12582916
  62.3 1.6 copy-start.6
  99.1 53.0 %all-to-all-start = ((bf16[4,512,512]{2,1,0:T(8,128)(2,1)}), bf16[4,512,512]{2,1,0:T(8,128)(2,1)}, u32[]{:S(2)}, u32[]{:S(2)}) async-start(bf16[4,512,512]{2,1,0:T(8,128)(2,1)} %get-tuple-element.13), calls=%async_computation | async-start | bytes 4194304 | tf_op jit(solution)/shard_map/all_to_all | solution.py:182
  103.6 0.9 copy-start.7
  104.5 52.3 %collective-permute-start.1 = (bf16[1024,256]{1,0:T(8,128)(2,1)}, bf16[1024,256]{1,0:T(8,128)(2,1)}, u32[]{:S(2)}, u32[]{:S(2)}) collective-permute-start(bf16[1024,256]{1,0:T(8,128)(2,1)} %pad_maximum_fusion.4), channel_id=1, source_target_pairs={{0,1},{1,0},{2,3},{3,2},{4,5},{5,4},{6,7},{7,6},{8,9},{9,8},{10,11... | collective-permute-start | bytes 1572872 | tf_op jit(solution)/shard_map/ppermute | solution.py:191
  155.3 1.0 copy-start.9
  155.5 1.3 copy-start.8
  156.7 2.0 %collective-permute-start = (bf16[1024,256]{1,0:T(8,128)(2,1)S(1)}, bf16[1024,256]{1,0:T(8,128)(2,1)S(1)}, u32[]{:S(2)}, u32[]{:S(2)}) collective-permute-start(bf16[1024,256]{1,0:T(8,128)(2,1)S(1)} %pad_maximum_fusion.3), channel_id=1, source_target_pairs={{0,1},{1,0},{2,3},{3,2},{4,5},{5,4},{6,7},{7,6},{8,9},{9,8},{10,11... | collective-permute-start | bytes 1572872 | tf_op jit(solution)/shard_map/ppermute | solution.py:191
Sparse Core Ops, SparseCore 0:
  10.2 48.6 all-gather.2
where the time goes:
time: 168 us
  waiting for transfers between devices  70 us (42%)
  Pallas kernels  58.1 us (35%)
  between operations  14.3 us (9%)
  local copies, waits for them, and re-layouts  13 us (8%)
  other arithmetic  8 us (5%)
  starting transfers between devices  4.55 us (3%)
    all_to_all x1, waiting for transfers between devices, per_device(): lax.all_to_all(outgoing, 'seq', split_axis=0, concat_axis=0, tiled=True)  47.6 us
    pallas_call x1, Pallas kernels, per_device(): pl.pallas_call(functools.partial(reply_kernel, shared), grid_spec=pltpu.P...  35.2 us
    pallas_call x1, Pallas kernels, per_device(): pl.pallas_call(functools.partial(prompt_kernel, shared), grid_spec=pltpu....  22.8 us
    all_gather x1, waiting for transfers between devices, per_device(): every = lax.all_gather(prompt_pair[None], 'seq', axis=0, tiled=True)  21.8 us
    unnamed x26, local copies, waits for them, and re-layouts  10.2 us
    all_to_all x1, starting transfers between devices, per_device(): lax.all_to_all(outgoing, 'seq', split_axis=0, concat_axis=0, tiled=True)  4.44 us
  transfers between devices with their start and end apart: 4, of which 3 were waited for; matrix products, arithmetic and copies ran while one was open for 4% of the time, Pallas kernels for 14%

commit v1 on v0

v1 whole, which is shorter than its diff:
```python
import functools
import math

import jax
import jax.numpy as jnp
from jax import lax
from jax.experimental import pallas as pl
from jax.experimental.pallas import tpu as pltpu
from jax.sharding import PartitionSpec as P

HQ = 64
KVH = 8
HD = 128
PROMPT = 512
RESP = 256
SCALE = 1.0 / math.sqrt(HD)
EXP2_SCALE = SCALE * math.log2(math.e)
ROW_ROW = (((1,), (1,)), ((), ()))
MESH = pl.DeviceIdType.MESH


def attend(query, grad, key, value, key_turned):
    extent, amount = key.shape[0], query.shape[0]
    scores = lax.dot_general(key, query, ROW_ROW, preferred_element_type=jnp.float32)
    grad_chance = lax.dot_general(value, grad, ROW_ROW, preferred_element_type=jnp.float32)
    key_index = lax.broadcasted_iota(jnp.int32, (amount, amount), 0)
    query_index = lax.broadcasted_iota(jnp.int32, (amount, amount), 1)
    last = jnp.where(key_index <= query_index, scores[extent - amount :], -jnp.inf)
    if extent > amount:
        scores = jnp.concatenate([scores[: extent - amount], last], axis=0)
    else:
        scores = last
    highest = jnp.max(scores, axis=0, keepdims=True)
    weights = jnp.exp2((scores - highest) * EXP2_SCALE)
    inverse = 1.0 / jnp.sum(weights, axis=0, keepdims=True)
    row_dot = jnp.sum(weights * grad_chance, axis=0, keepdims=True) * inverse
    chances = (weights * inverse).astype(jnp.bfloat16)
    grad_score = chances * (grad_chance - row_dot).astype(jnp.bfloat16)
    key_term = jnp.dot(grad_score, query, preferred_element_type=jnp.float32)
    value_term = jnp.dot(chances, grad, preferred_element_type=jnp.float32)
    query_turned = jnp.dot(key_turned, grad_score, preferred_element_type=jnp.float32)
    query_grad = (query_turned.T * SCALE).astype(jnp.bfloat16)
    return query_grad, key_term, value_term


def fused(plan, table, q_hbm, g_hbm, k_hbm, v_hbm, dq_hbm, dk_hbm, dv_hbm, *scratch):
    count, used, shared, kv_local = plan
    (q, g, dq, own, key_turned, joined, joined_turned, prompt_acc, reply_acc, final, load_sem, store_sem) = scratch[:12]
    (gather_send, gather_recv, back_send, back_recv, sub_send, sub_recv) = scratch[12:18]
    every = scratch[18 : 18 + used]
    outgoing = scratch[18 + used : 18 + 2 * used]
    arrived = scratch[18 + 2 * used : 18 + 3 * used]
    partner_terms = scratch[18 + 3 * used :]
    me = lax.axis_index("seq")
    sub = lax.axis_index("sub")
    split = used != kv_local
    first_head = sub * used if split else 0
    width = shared * HD
    peers = [lax.rem(me + step, count) for step in range(count)]
    kv_hbm, dkv_hbm = (k_hbm, v_hbm), (dk_hbm, dv_hbm)

    def columns(head):
        return pl.ds(pl.multiple_of((first_head + head) * HD, HD), HD)

    loads = {}
    for head in range(used):
        for which in range(2):
            copy = pltpu.make_async_copy(
                kv_hbm[which].at[:, columns(head)], own.at[head, which], load_sem.at[head, 4 + which]
            )
            copy.start()
            loads[head, 4 + which] = copy
    for head in range(used):
        for half in range(2):
            rows = pl.ds(half * PROMPT, PROMPT)
            place = pl.ds(head * width, width)
            for which, source, target in ((0, q_hbm, q), (1, g_hbm, g)):
                copy = pltpu.make_async_copy(
                    source.at[rows, place], target.at[rows, place], load_sem.at[head, 2 * half + which]
                )
                copy.start()
                loads[head, 2 * half + which] = copy

    barrier = pltpu.get_barrier_semaphore()
    for peer in peers[1:]:
        pl.semaphore_signal(barrier, inc=1, device_id={"seq": peer}, device_id_type=MESH)
    pl.semaphore_signal(barrier, inc=1, device_id={"sub": 1 - sub}, device_id_type=MESH)
    pl.semaphore_wait(barrier, count)

    gathers = []
    for head in range(used):
        group = []
        for which in range(2):
            for step in range(1, count):
                copy = pltpu.make_async_remote_copy(
                    src_ref=kv_hbm[which].at[pl.ds(0, PROMPT), columns(head)],
                    dst_ref=every[head].at[me, which],
                    send_sem=gather_send.at[head, which, step],
                    recv_sem=gather_recv.at[head, which, step],
                    device_id={"seq": peers[step]},
                    device_id_type=MESH,
                )
                copy.start()
                group.append(copy)
        gathers.append(group)

    prompt_acc[...] = jnp.zeros_like(prompt_acc)

    def head_place(head, member):
        return pl.ds(pl.multiple_of(head * width + member * HD, HD), HD)

    def prompt_work(head, begin, finish):
        if begin == 0:
            for index in (4, 5, 0, 1):
                loads[head, index].wait()
            key_turned[...] = own[head, 0, :PROMPT].T

        @pl.loop(begin, finish)
        def _(member):
            place = head_place(head, member)
            for start in range(0, PROMPT, RESP):
                rows, seen = pl.ds(start, RESP), pl.ds(0, start + RESP)
                dq[rows, place], key_term, value_term = attend(
                    q[rows, place], g[rows, place], own[head, 0, seen], own[head, 1, seen], key_turned[:, seen]
                )
                prompt_acc[head, 0, seen] += key_term
                prompt_acc[head, 1, seen] += value_term

        return store_query(head, 0) if finish == shared else None

    def store_query(head, half):
        rows, place = pl.ds(half * PROMPT, PROMPT), pl.ds(head * width, width)
        copy = pltpu.make_async_copy(
            dq.at[rows, place], dq_hbm.at[rows, place], store_sem.at[head, half]
        )
        copy.start()
        return copy

    def reply_work(head):
        for which in range(2):
            every[head][me, which] = own[head, which, :PROMPT]
        for copy in gathers[head]:
            copy.wait()
        for slot in range(2):
            for which in range(2):
                joined[slot, which, :PROMPT] = every[head][table[slot], which]
                joined[slot, which, PROMPT:] = own[head, which, PROMPT + slot * RESP : PROMPT + (slot + 1) * RESP]
            joined_turned[slot] = joined[slot, 0].T
        loads[head, 2].wait()
        loads[head, 3].wait()
        reply_acc[...] = jnp.zeros_like(reply_acc)
        live_index = lax.broadcasted_iota(jnp.int32, (RESP, 1), 0)

        @pl.loop(0, shared)
        def _(member):
            place = head_place(head, member)
            for slot in range(2):
                rows = pl.ds(PROMPT + slot * RESP, RESP)
                live = jnp.where(live_index < table[2 + slot], g[rows, place], jnp.zeros((), jnp.bfloat16))
                dq[rows, place], key_term, value_term = attend(
                    q[rows, place], live, joined[slot, 0], joined[slot, 1], joined_turned[slot]
                )
                reply_acc[slot, 0] += key_term
                reply_acc[slot, 1] += value_term

        copies = []
        for step in range(count):
            for which in range(2):
                total = jnp.where(table[0] == peers[step], reply_acc[0, which, :PROMPT], 0.0) + jnp.where(
                    table[1] == peers[step], reply_acc[1, which, :PROMPT], 0.0
                )
                if step == 0:
                    prompt_acc[head, which] += total
                else:
                    factor = (SCALE, 1.0)[which]
                    outgoing[head][step, which] = (total * factor).astype(jnp.bfloat16)
            if step:
                copy = pltpu.make_async_remote_copy(
                    src_ref=outgoing[head].at[step],
                    dst_ref=arrived[head].at[step],
                    send_sem=back_send.at[head, step],
                    recv_sem=back_recv.at[head, step],
                    device_id={"seq": peers[step]},
                    device_id_type=MESH,
                )
                copy.start()
                copies.append(copy)
        for which in range(2):
            for slot in range(2):
                total = reply_acc[slot, which, PROMPT:] * (SCALE, 1.0)[which]
                final[head, which, PROMPT + slot * RESP : PROMPT + (slot + 1) * RESP] = total.astype(jnp.bfloat16)
        return copies, store_query(head, 1), share(head, 1)

    def share(head, half):
        rows = pl.ds(half * PROMPT, PROMPT)
        copies = []
        for which in range(2):
            source = final.at[head, which, rows]
            target = dkv_hbm[which].at[rows, columns(head)] if split else partner_terms[0].at[head, which, rows]
            remote = pltpu.make_async_remote_copy(
                src_ref=source,
                dst_ref=target,
                send_sem=sub_send.at[head, which, half],
                recv_sem=sub_recv.at[head, which, half],
                device_id={"sub": 1 - sub},
                device_id_type=MESH,
            )
            remote.start()
            copies.append(remote)
            if split:
                local = pltpu.make_async_copy(source, target, store_sem.at[head, 2 + 2 * which + half])
                local.start()
                copies.append(local)
        return copies

    pending = []
    early = shared // 2 if used > 1 else 0
    pending.append(prompt_work(0, 0, shared))
    if early:
        prompt_work(1, 0, early)
    backs = []
    for head in range(used):
        copies, stored, shares = reply_work(head)
        backs.append(copies)
        pending.append(stored)
        pending.extend(shares)
    for head in range(1, used):
        pending.append(prompt_work(head, early if head == 1 else 0, shared))
    for head in range(used):
        for copy in backs[head]:
            copy.wait()
        for which in range(2):
            total = prompt_acc[head, which] * (SCALE, 1.0)[which]
            for step in range(1, count):
                total += arrived[head][step, which].astype(jnp.float32)
            final[head, which, :PROMPT] = total.astype(jnp.bfloat16)
        pending.extend(share(head, 0))
    for copy in pending:
        copy.wait()
    if not split:
        for head in range(used):
            for which in range(2):
                mine = final[head, which].astype(jnp.float32)
                both = mine + partner_terms[0][head, which].astype(jnp.float32)
                final[head, which] = both.astype(jnp.bfloat16)
                copy = pltpu.make_async_copy(
                    final.at[head, which], dkv_hbm[which].at[:, columns(head)], store_sem.at[head, 2 + which]
                )
                copy.start()
                copy.wait()


def per_device(queries, keys, values, out_grad, prompt_group, slot_group, resp_len):
    seq_count = lax.axis_size("seq")
    local_heads = queries.shape[1] // HD
    kv_local = keys.shape[1] // HD
    used = max(local_heads // (HQ // KVH), 1)
    shared = local_heads // used
    total_rows = queries.shape[0]
    peers = jnp.arange(seq_count, dtype=jnp.int32)
    owners = jnp.sum(
        peers[:, None] * (prompt_group[:, None] == peers[None, :]).astype(jnp.int32), axis=0
    )
    own_index = lax.axis_index("seq")
    my_slots = jnp.sum(slot_group * (peers[:, None] == own_index).astype(jnp.int32), axis=0)
    my_owner = jnp.sum(
        owners[None, :] * (my_slots[:, None] == peers[None, :]).astype(jnp.int32), axis=1
    )
    table = jnp.concatenate([my_owner, resp_len[0]]).astype(jnp.int32)
    anywhere = pl.BlockSpec(memory_space=pl.ANY)
    bf16, f32 = jnp.bfloat16, jnp.float32
    dma = pltpu.SemaphoreType.DMA
    exchanged = [pltpu.VMEM((seq_count, 2, PROMPT, HD), bf16)] * (3 * used)
    partner = [] if used != kv_local else [pltpu.VMEM((used, 2, total_rows, HD), bf16)]
    return pl.pallas_call(
        functools.partial(fused, (seq_count, used, shared, kv_local)),
        in_specs=[pl.BlockSpec(memory_space=pltpu.SMEM)] + [anywhere] * 4,
        out_specs=[anywhere] * 3,
        out_shape=[jax.ShapeDtypeStruct(array.shape, bf16) for array in (queries, keys, values)],
        scratch_shapes=[
            pltpu.VMEM(queries.shape, bf16),
            pltpu.VMEM(queries.shape, bf16),
            pltpu.VMEM(queries.shape, bf16),
            pltpu.VMEM((used, 2, total_rows, HD), bf16),
            pltpu.VMEM((HD, PROMPT), bf16),
            pltpu.VMEM((2, 2, PROMPT + RESP, HD), bf16),
            pltpu.VMEM((2, HD, PROMPT + RESP), bf16),
            pltpu.VMEM((used, 2, PROMPT, HD), f32),
            pltpu.VMEM((2, 2, PROMPT + RESP, HD), f32),
            pltpu.VMEM((used, 2, total_rows, HD), bf16),
            dma((used, 6)),
            dma((used, 6)),
            dma((used, 2, seq_count)),
            dma((used, 2, seq_count)),
            dma((used, seq_count)),
            dma((used, seq_count)),
            dma((used, 2, 2)),
            dma((used, 2, 2)),
        ]
        + exchanged
        + partner,
        compiler_params=pltpu.CompilerParams(
            collective_id=0, has_side_effects=True, vmem_limit_bytes=56 * 1024 * 1024
        ),
    )(table, queries, out_grad, keys, values)


def solution(mesh):
    placed = (
        P(("parts", "seq"), ("head", "sub")),
        P(("parts", "seq"), "head"),
        P(("parts", "seq"), "head"),
        P(("parts", "seq"), ("head", "sub")),
        P("parts"),
        P("parts", None),
        P(("parts", "seq"), None),
    )
    return jax.shard_map(
        per_device,
        mesh=mesh,
        in_specs=placed,
        out_specs=(
            P(("parts", "seq"), ("head", "sub")),
            P(("parts", "seq"), "head"),
            P(("parts", "seq"), "head"),
        ),
        check_vma=False,
    )
```

time: 168 us -> 111 us (0.66)
  the two profiles are of different devices: /device:TPU:0 before, /device:TPU:25 now
where the time goes in v1:
time: 111 us; the launch traced here: 110 us
  Pallas kernels  99.9 us (90%)
  local copies, waits for them, and re-layouts  6.88 us (6%)
  other arithmetic  2.97 us (3%)
    pallas_call x1, Pallas kernels, per_device(): pl.pallas_call(functools.partial(fused, (seq_count, used, shared, kv_loca...  99.9 us
    unnamed x7, local copies, waits for them, and re-layouts  6.88 us

profile of v1, /device:TPU:25, one launch (start us, length us, event | category | flops | bytes accessed | tf_op | source)
XLA Modules:
  0.0 110.4 jit_solution(14718195590440578811)
XLA Ops:
  0.6 0.8 multiply_reduce_fusion
  1.4 0.7 select_reduce_fusion
  2.2 0.2 fusion
  2.4 1.2 %pad_add_fusion.table = s32[4]{0:T(128)} fusion(s32[2]{0:T(128)} %bitcast.1, s32[2]{0:T(128)S(1)} %fusion), kind=kLoop, calls=%fused_computation.6 | loop fusion | flops 4 | bytes 32 | tf_op jit(solution)/shard_map/concatenate | solution.py:269
  3.6 99.9 %shard_map.94 = (bf16[1024,2048]{1,0:T(8,128)(2,1)}, bf16[1024,512]{1,0:T(8,128)(2,1)}, bf16[1024,512]{1,0:T(8,128)(2,1)}) custom-call(s32[4]{0:T(128)} %pad_add_fusion.table, bf16[1024,2048]{1,0:T(8,128)(2,1)} %q_hbm.1, bf16[1024,2048]{1,0:T(8,128)(2,1)} %g_hbm.1, bf16[1024,512]{1,0:T(8,128)(2,1)} %k_hbm.1, bf16[1024,512]{1,0:T(8,128)(2,1)} %v_hbm.1), custom_call_target="tpu_custom_call" | custom-call | tf_op jit(solution)/shard_map/pallas_call | solution.py:275
  103.5 0.0 copy-start.1
  103.5 0.0 copy-start
  103.6 4.9 %copy.13 = bf16[1024,2048]{1,0:T(8,128)(2,1)} copy(bf16[1024,2048]{1,0:T(8,128)(2,1)} %get-tuple-element.6) | data formatting | bytes 8388608
  108.5 0.0 copy-done.1
  108.5 1.0 copy.14
  109.5 0.0 copy-done
  109.5 1.0 copy.15
  (1 shorter events, 0.0 us)
Async XLA Ops:
  103.5 5.0 %copy-start.1 = (bf16[1024,512]{1,0:T(8,128)(2,1)S(1)}, bf16[1024,512]{1,0:T(8,128)(2,1)}, u32[]{:S(2)}) copy-start(bf16[1024,512]{1,0:T(8,128)(2,1)} %get-tuple-element.7) | copy-start | bytes 3145732
  103.5 5.9 %copy-start = (bf16[1024,512]{1,0:T(8,128)(2,1)S(1)}, bf16[1024,512]{1,0:T(8,128)(2,1)}, u32[]{:S(2)}) copy-start(bf16[1024,512]{1,0:T(8,128)(2,1)} %get-tuple-element.8) | copy-start | bytes 3145732

commit v2 on v1

--- a/solution.py
+++ b/solution.py
@@ -14,6 +14,7 @@
 PROMPT = 512
 RESP = 256
 SCALE = 1.0 / math.sqrt(HD)
+EARLY = 2
 EXP2_SCALE = SCALE * math.log2(math.e)
 ROW_ROW = (((1,), (1,)), ((), ()))
 MESH = pl.DeviceIdType.MESH
@@ -48,15 +49,13 @@
     (q, g, dq, own, key_turned, joined, joined_turned, prompt_acc, reply_acc, final, load_sem, store_sem) = scratch[:12]
     (gather_send, gather_recv, back_send, back_recv, sub_send, sub_recv) = scratch[12:18]
     every = scratch[18 : 18 + used]
-    outgoing = scratch[18 + used : 18 + 2 * used]
-    arrived = scratch[18 + 2 * used : 18 + 3 * used]
-    partner_terms = scratch[18 + 3 * used :]
+    terms, sent, arrived = scratch[18 + used : 21 + used]
+    partner_terms = scratch[21 + used :]
     me = lax.axis_index("seq")
     sub = lax.axis_index("sub")
     split = used != kv_local
     first_head = sub * used if split else 0
     width = shared * HD
-    peers = [lax.rem(me + step, count) for step in range(count)]
     kv_hbm, dkv_hbm = (k_hbm, v_hbm), (dk_hbm, dv_hbm)
 
     def columns(head):
@@ -82,41 +81,167 @@
                 loads[head, 2 * half + which] = copy
 
     barrier = pltpu.get_barrier_semaphore()
-    for peer in peers[1:]:
-        pl.semaphore_signal(barrier, inc=1, device_id={"seq": peer}, device_id_type=MESH)
+    ways = [(0, me, 1), (1, count - 1 - me, -1)]
+    for _, rank, sign in ways:
+
+        @pl.when(rank < count - 1)
+        def _():
+            pl.semaphore_signal(barrier, inc=1, device_id={"seq": me + sign}, device_id_type=MESH)
+
     pl.semaphore_signal(barrier, inc=1, device_id={"sub": 1 - sub}, device_id_type=MESH)
-    pl.semaphore_wait(barrier, count)
-
-    gathers = []
+    near = jnp.where(me > 0, 1, 0) + jnp.where(me < count - 1, 1, 0)
+    pl.semaphore_wait(barrier, near + 1)
+
+    def gather_copy(head, way, sign, tick, first):
+        block = me - sign * tick
+        return pltpu.make_async_remote_copy(
+            src_ref=own.at[head, :, pl.ds(0, PROMPT)] if first else every[head].at[block],
+            dst_ref=every[head].at[block],
+            send_sem=gather_send.at[head, way, tick],
+            recv_sem=gather_recv.at[head, way, tick],
+            device_id={"seq": me + sign},
+            device_id_type=MESH,
+        )
+
+    def gather_arrival(head, way, sign, tick):
+        block = every[head].at[me - sign * tick]
+        return pltpu.make_async_remote_copy(
+            src_ref=block,
+            dst_ref=block,
+            send_sem=gather_send.at[head, way, tick],
+            recv_sem=gather_recv.at[head, way, tick - 1],
+            device_id={"seq": me - sign},
+            device_id_type=MESH,
+        )
+
+    def gather_first(head):
+        for way, rank, sign in ways:
+
+            @pl.when(rank < count - 1)
+            def _():
+                gather_copy(head, way, sign, 0, True).start()
+
+    def gather_tick(head, tick):
+        for way, rank, sign in ways:
+
+            @pl.when(tick <= rank)
+            def _():
+                gather_arrival(head, way, sign, tick).wait_recv()
+
+            @pl.when((tick <= rank) & (rank < count - 1))
+            def _():
+                gather_copy(head, way, sign, tick, False).start()
+
+    def back_copy(head, way, sign, tick):
+        return pltpu.make_async_remote_copy(
+            src_ref=sent.at[head, way, tick],
+            dst_ref=arrived.at[head, way, tick],
+            send_sem=back_send.at[head, way, tick],
+            recv_sem=back_recv.at[head, way, tick],
+            device_id={"seq": me + sign},
+            device_id_type=MESH,
+        )
+
+    def term_for(head, which, target):
+        return jnp.where(table[0] == target, terms[head, 0, which].astype(jnp.float32), 0.0) + jnp.where(
+            table[1] == target, terms[head, 1, which].astype(jnp.float32), 0.0
+        )
+
+    def back_first(head):
+        for way, rank, sign in ways:
+
+            @pl.when(rank == 0)
+            def _():
+                for which in range(2):
+                    total = term_for(head, which, me + sign * (count - 1))
+                    sent[head, way, 0, which] = total.astype(jnp.bfloat16)
+                back_copy(head, way, sign, 0).start()
+
+    def back_tick(head, tick):
+        for way, rank, sign in ways:
+            target = me + sign * (count - 1 - tick)
+
+            @pl.when((tick >= rank) & (rank > 0))
+            def _():
+                pltpu.make_async_remote_copy(
+                    src_ref=arrived.at[head, way, tick - 1],
+                    dst_ref=arrived.at[head, way, tick - 1],
+                    send_sem=back_send.at[head, way, tick],
+                    recv_sem=back_recv.at[head, way, tick - 1],
+                    device_id={"seq": me - sign},
+                    device_id_type=MESH,
+                ).wait_recv()
+
+            @pl.when((tick >= rank) & (rank > 0) & (tick < count - 1))
+            def _():
+                for which in range(2):
+                    total = term_for(head, which, target) + arrived[head, way, tick - 1, which].astype(jnp.float32)
+                    sent[head, way, tick, which] = total.astype(jnp.bfloat16)
+                back_copy(head, way, sign, tick).start()
+
+            @pl.when((rank == 0) & (tick < count - 1))
+            def _():
+                for which in range(2):
+                    sent[head, way, tick, which] = term_for(head, which, target).astype(jnp.bfloat16)
+                back_copy(head, way, sign, tick).start()
+
+            @pl.when((rank > 0) & (tick == count - 1))
+            def _():
+                for which in range(2):
+                    prompt_acc[head, which] += arrived[head, way, count - 2, which].astype(jnp.float32)
+
+    def finish_sends():
+        for head in range(used):
+            for way, rank, sign in ways:
+
+                @pl.loop(0, count - 1)
+                def _(tick):
+                    @pl.when((tick <= rank) & (rank < count - 1))
+                    def _():
+                        gather_copy(head, way, sign, tick, False).wait_send()
+
+                    @pl.when(tick >= rank)
+                    def _():
+                        back_copy(head, way, sign, tick).wait_send()
+
+    def members(begin, finish, work, ticker=None, interval=1):
+        @pl.loop(begin, finish)
+        def _(member):
+            work(member)
+            if ticker is not None:
+                passed = member - begin + 1
+                tick = passed // interval
+
+                @pl.when((passed % interval == 0) & (tick < count))
+                def _():
+                    ticker(tick)
+
+        return 1 + ((finish - begin) // interval if ticker is not None else 0)
+
+    def flush(ticker, tick):
+        if tick < count:
+
+            @pl.loop(tick, count)
+            def _(later):
+                ticker(later)
+
     for head in range(used):
-        group = []
-        for which in range(2):
-            for step in range(1, count):
-                copy = pltpu.make_async_remote_copy(
-                    src_ref=kv_hbm[which].at[pl.ds(0, PROMPT), columns(head)],
-                    dst_ref=every[head].at[me, which],
-                    send_sem=gather_send.at[head, which, step],
-                    recv_sem=gather_recv.at[head, which, step],
-                    device_id={"seq": peers[step]},
-                    device_id_type=MESH,
-                )
-                copy.start()
-                group.append(copy)
-        gathers.append(group)
-
+        loads[head, 4].wait()
+        loads[head, 5].wait()
+        if head == 0:
+            gather_first(0)
     prompt_acc[...] = jnp.zeros_like(prompt_acc)
 
     def head_place(head, member):
         return pl.ds(pl.multiple_of(head * width + member * HD, HD), HD)
 
-    def prompt_work(head, begin, finish):
+    def prompt_work(head, begin, finish, ticker=None, interval=1):
         if begin == 0:
-            for index in (4, 5, 0, 1):
+            for index in (0, 1):
                 loads[head, index].wait()
             key_turned[...] = own[head, 0, :PROMPT].T
 
-        @pl.loop(begin, finish)
-        def _(member):
+        def work(member):
             place = head_place(head, member)
             for start in range(0, PROMPT, RESP):
                 rows, seen = pl.ds(start, RESP), pl.ds(0, start + RESP)
@@ -126,7 +251,10 @@
                 prompt_acc[head, 0, seen] += key_term
                 prompt_acc[head, 1, seen] += value_term
 
-        return store_query(head, 0) if finish == shared else None
+        tick = members(begin, finish, work, ticker, interval)
+        if finish == shared:
+            pending.append(store_query(head, 0))
+        return tick
 
     def store_query(head, half):
         rows, place = pl.ds(half * PROMPT, PROMPT), pl.ds(head * width, width)
@@ -136,11 +264,9 @@
         copy.start()
         return copy
 
-    def reply_work(head):
+    def reply_work(head, ticker=None, interval=1):
         for which in range(2):
             every[head][me, which] = own[head, which, :PROMPT]
-        for copy in gathers[head]:
-            copy.wait()
         for slot in range(2):
             for which in range(2):
                 joined[slot, which, :PROMPT] = every[head][table[slot], which]
@@ -151,8 +277,7 @@
         reply_acc[...] = jnp.zeros_like(reply_acc)
         live_index = lax.broadcasted_iota(jnp.int32, (RESP, 1), 0)
 
-        @pl.loop(0, shared)
-        def _(member):
+        def work(member):
             place = head_place(head, member)
             for slot in range(2):
                 rows = pl.ds(PROMPT + slot * RESP, RESP)
@@ -163,33 +288,20 @@
                 reply_acc[slot, 0] += key_term
                 reply_acc[slot, 1] += value_term
 
-        copies = []
-        for step in range(count):
-            for which in range(2):
-                total = jnp.where(table[0] == peers[step], reply_acc[0, which, :PROMPT], 0.0) + jnp.where(
-                    table[1] == peers[step], reply_acc[1, which, :PROMPT], 0.0
-                )
-                if step == 0:
-                    prompt_acc[head, which] += total
-                else:
-                    factor = (SCALE, 1.0)[which]
-                    outgoing[head][step, which] = (total * factor).astype(jnp.bfloat16)
-            if step:
-                copy = pltpu.make_async_remote_copy(
-                    src_ref=outgoing[head].at[step],
-                    dst_ref=arrived[head].at[step],
-                    send_sem=back_send.at[head, step],
-                    recv_sem=back_recv.at[head, step],
-                    device_id={"seq": peers[step]},
-                    device_id_type=MESH,
-                )
-                copy.start()
-                copies.append(copy)
+        tick = members(0, shared, work, ticker, interval)
+        for which in range(2):
+            for slot in range(2):
+                total = reply_acc[slot, which, :PROMPT]
+                terms[head, slot, which] = total.astype(jnp.bfloat16)
+                prompt_acc[head, which] += jnp.where(table[slot] == me, total, 0.0)
+        back_first(head)
         for which in range(2):
             for slot in range(2):
                 total = reply_acc[slot, which, PROMPT:] * (SCALE, 1.0)[which]
                 final[head, which, PROMPT + slot * RESP : PROMPT + (slot + 1) * RESP] = total.astype(jnp.bfloat16)
-        return copies, store_query(head, 1), share(head, 1)
+        pending.append(store_query(head, 1))
+        pending.extend(share(head, 1))
+        return tick
 
     def share(head, half):
         rows = pl.ds(half * PROMPT, PROMPT)
@@ -214,25 +326,40 @@
         return copies
 
     pending = []
-    early = shared // 2 if used > 1 else 0
-    pending.append(prompt_work(0, 0, shared))
-    if early:
-        prompt_work(1, 0, early)
-    backs = []
+
+    def gather_of(head):
+        return lambda tick: gather_tick(head, tick)
+
+    def back_of(head):
+        return lambda tick: back_tick(head, tick)
+
+    early = EARLY if used > 1 else 0
+    tick = prompt_work(0, 0, shared, gather_of(0), 4)
+    if used > 1:
+        gather_first(1)
+        if early:
+            prompt_work(1, 0, early)
+    flush(gather_of(0), tick)
     for head in range(used):
-        copies, stored, shares = reply_work(head)
-        backs.append(copies)
-        pending.append(stored)
-        pending.extend(shares)
+        if head == 0 and used > 1:
+            flush(gather_of(1), reply_work(0, gather_of(1), 2))
+        elif head == 0:
+            reply_work(0)
+        else:
+            if head > 1:
+                gather_first(head)
+                flush(gather_of(head), 1)
+            flush(back_of(head - 1), reply_work(head, back_of(head - 1), 2))
+    tick = 1
     for head in range(1, used):
-        pending.append(prompt_work(head, early if head == 1 else 0, shared))
+        ticker = back_of(used - 1) if head == 1 else None
+        passed = prompt_work(head, early if head == 1 else 0, shared, ticker, 3)
+        tick = passed if head == 1 else tick
+    flush(back_of(used - 1), tick)
+    finish_sends()
     for head in range(used):
-        for copy in backs[head]:
-            copy.wait()
         for which in range(2):
             total = prompt_acc[head, which] * (SCALE, 1.0)[which]
-            for step in range(1, count):
-                total += arrived[head][step, which].astype(jnp.float32)
             final[head, which, :PROMPT] = total.astype(jnp.bfloat16)
         pending.extend(share(head, 0))
     for copy in pending:
@@ -270,7 +397,9 @@
     anywhere = pl.BlockSpec(memory_space=pl.ANY)
     bf16, f32 = jnp.bfloat16, jnp.float32
     dma = pltpu.SemaphoreType.DMA
-    exchanged = [pltpu.VMEM((seq_count, 2, PROMPT, HD), bf16)] * (3 * used)
+    exchanged = [pltpu.VMEM((seq_count, 2, PROMPT, HD), bf16)] * used
+    exchanged += [pltpu.VMEM((used, 2, 2, PROMPT, HD), bf16)]
+    exchanged += [pltpu.VMEM((used, 2, seq_count, 2, PROMPT, HD), bf16)] * 2
     partner = [] if used != kv_local else [pltpu.VMEM((used, 2, total_rows, HD), bf16)]
     return pl.pallas_call(
         functools.partial(fused, (seq_count, used, shared, kv_local)),
@@ -292,8 +421,8 @@
             dma((used, 6)),
             dma((used, 2, seq_count)),
             dma((used, 2, seq_count)),
-            dma((used, seq_count)),
-            dma((used, seq_count)),
+            dma((used, 2, seq_count)),
+            dma((used, 2, seq_count)),
             dma((used, 2, 2)),
             dma((used, 2, 2)),
         ]

time: 111 us -> 102 us (0.919)
  the two profiles are of different devices: /device:TPU:25 before, /device:TPU:0 now
where the time goes in v2:
time: 102 us
  Pallas kernels  91.2 us (89%)
  local copies, waits for them, and re-layouts  6.88 us (7%)
  other arithmetic  2.97 us (3%)
    pallas_call x1, Pallas kernels, per_device(): pl.pallas_call(functools.partial(fused, (seq_count, used, shared, kv_loca...  91.2 us
    unnamed x7, local copies, waits for them, and re-layouts  6.88 us

profile of v2, /device:TPU:0, one launch (start us, length us, event | category | flops | bytes accessed | tf_op | source)
XLA Modules:
  0.0 101.7 jit_solution(12910069625847775471)
XLA Ops:
  0.6 0.8 multiply_reduce_fusion
  1.4 0.7 select_reduce_fusion
  2.2 0.2 fusion
  2.4 1.2 %pad_add_fusion.table = s32[4]{0:T(128)} fusion(s32[2]{0:T(128)} %bitcast.1, s32[2]{0:T(128)S(1)} %fusion), kind=kLoop, calls=%fused_computation.6 | loop fusion | flops 4 | bytes 32 | tf_op jit(solution)/shard_map/concatenate | solution.py:396
  3.6 91.2 %shard_map.94 = (bf16[1024,2048]{1,0:T(8,128)(2,1)}, bf16[1024,512]{1,0:T(8,128)(2,1)}, bf16[1024,512]{1,0:T(8,128)(2,1)}) custom-call(s32[4]{0:T(128)} %pad_add_fusion.table, bf16[1024,2048]{1,0:T(8,128)(2,1)} %q_hbm.1, bf16[1024,2048]{1,0:T(8,128)(2,1)} %g_hbm.1, bf16[1024,512]{1,0:T(8,128)(2,1)} %k_hbm.1, bf16[1024,512]{1,0:T(8,128)(2,1)} %v_hbm.1), custom_call_target="tpu_custom_call" | custom-call | tf_op jit(solution)/shard_map/pallas_call | solution.py:404
  94.8 0.0 copy-start.1
  94.8 0.0 copy-start
  94.8 4.9 %copy.13 = bf16[1024,2048]{1,0:T(8,128)(2,1)} copy(bf16[1024,2048]{1,0:T(8,128)(2,1)} %get-tuple-element.6) | data formatting | bytes 8388608
  99.8 0.0 copy-done.1
  99.8 1.0 copy.14
  100.7 0.0 copy-done
  100.7 1.0 copy.15
  (1 shorter events, 0.0 us)
Async XLA Ops:
  94.8 5.0 %copy-start.1 = (bf16[1024,512]{1,0:T(8,128)(2,1)S(1)}, bf16[1024,512]{1,0:T(8,128)(2,1)}, u32[]{:S(2)}) copy-start(bf16[1024,512]{1,0:T(8,128)(2,1)} %get-tuple-element.7) | copy-start | bytes 3145732
  94.8 5.9 %copy-start = (bf16[1024,512]{1,0:T(8,128)(2,1)S(1)}, bf16[1024,512]{1,0:T(8,128)(2,1)}, u32[]{:S(2)}) copy-start(bf16[1024,512]{1,0:T(8,128)(2,1)} %get-tuple-element.8) | copy-start | bytes 3145732
